TPU v7x, 128 devices: a whole 4x4x4 slice. The times are simulated.
128 devices in a mesh: gx: 8 (over x, core), gy: 16 (over y, z).
Axes of the slice: x: 4, y: 4, z: 4, core: 2. Of those that a mesh axis runs over, the one named last changes fastest.
Arguments:
- charges: bfloat16 [128, 8192, 128], P(('gx', 'gy')), may hold values from -6 to 6
- leaf_slot: int32 [128, 8192], P(('gx', 'gy')), may hold values from 0 to 8191, each once within a row
- node_offset: bfloat16 [128, 2, 8192], P(('gx', 'gy')), may hold values from -3.140625 to 3.140625
- lagrange: bfloat16 [2, 2, 2, 64, 64], replicated, may hold values from -0.375 to 0.375
- evaluate: bfloat16 [2, 64, 64], replicated, may hold values from -0.5 to 0.5
Outputs:
- target_field: bfloat16 [8192, 128, 128], P(('gx', 'gy'))
Inputs may be any that keep to these rules, and one draw needn't show every extreme that they name: Each block's row leaf_slot[b] is a permutation of 0 to 8191.
All inputs are finite; a program needn't handle non-finite values.
Results may differ from a plain program's by a relative error of at most 0.035.
Values may be sent and summed in bfloat16 or wider, within the bound.
A program may use at most 128 MiB of HBM per device.

v0:
```python
import math

import jax
import jax.numpy as jnp
from jax import lax
from jax.sharding import PartitionSpec as P


def partner_2(block, axis, bit):
    count = lax.axis_size(axis)
    route = []
    for low in range(count):
        high = low | 1 << bit
        if high != low and high < count:
            route += [(low, high), (high, low)]
    return lax.ppermute(block, axis, route)


def real_form(complex_parts):
    real_part = complex_parts[..., 0, :, :]
    imag_part = complex_parts[..., 1, :, :]
    upper = jnp.concatenate([real_part, imag_part], axis=-1)
    lower = jnp.concatenate([-imag_part, real_part], axis=-1)
    return jnp.concatenate([upper, lower], axis=-2)


def turn(current, offsets, factor):
    half_width = current.shape[-1] // 2
    side_count = math.isqrt(half_width)
    positions = jnp.arange(side_count, dtype=jnp.float32)
    chebyshev = jnp.cos(math.pi * (2.0 * positions + 1.0) / (2.0 * side_count))
    row_nodes = jnp.repeat(chebyshev, side_count)
    col_nodes = jnp.tile(chebyshev, side_count)
    first_term = offsets[..., 0, :, None].astype(jnp.float32) * row_nodes
    second = offsets[..., 1, :, None].astype(jnp.float32) * col_nodes
    angles = (first_term + second) * factor
    cosine = jnp.cos(angles)
    sine_part = jnp.sin(angles)
    real_part = current[..., :half_width]
    imag_part = current[..., half_width:]
    return jnp.concatenate(
        [cosine * real_part - sine_part * imag_part, sine_part * real_part + cosine * imag_part],
        axis=-1,
    ).astype(jnp.bfloat16)


def reversed_index(bit_count):
    positions = jnp.arange(1 << bit_count, dtype=jnp.int32)
    result = jnp.zeros_like(positions)
    for place in range(bit_count):
        result = result + (positions >> place & 1) * (1 << bit_count - 1 - place)
    return result


def merge_pair(phased, partner, mixing, child_bit):
    columns = lax.dynamic_index_in_dim(mixing, child_bit, axis=1, keepdims=False)
    own_matrix = lax.dynamic_index_in_dim(columns, child_bit, axis=0, keepdims=False)
    far_matrix = lax.dynamic_index_in_dim(columns, 1 - child_bit, axis=0, keepdims=False)
    return jnp.dot(phased, own_matrix, preferred_element_type=jnp.float32) + jnp.dot(
        partner, far_matrix, preferred_element_type=jnp.float32
    )


def body(charges, leaf_slot, node_offset, lagrange, evaluate):
    row_count = charges.shape[1]
    width = charges.shape[2]
    local_bits = row_count.bit_length() - 1
    inner_count = lax.axis_size("gy")
    outer_count = lax.axis_size("gx")
    inner_bits = inner_count.bit_length() - 1
    outer_bits = outer_count.bit_length() - 1
    level_count = local_bits + inner_bits + outer_bits
    block_count = inner_count * outer_count
    share_rows = row_count // block_count
    mixing = real_form(lagrange)
    flipped = reversed_index(local_bits)
    slots = jnp.take(leaf_slot[0], flipped, axis=0)
    current = jnp.take(charges[0], slots, axis=0).astype(jnp.float32)
    offsets = jnp.take(node_offset[0], flipped, axis=1)
    storage = jnp.arange(row_count, dtype=jnp.int32)
    rotation = storage % 2 * (row_count // 2) + storage // 2

    def local_level(level_index, carried):
        weights_now, offsets_now = carried
        phased = turn(weights_now, offsets_now, (level_index + 1).astype(jnp.float32))
        paired = phased.reshape(2, row_count // 2, width)
        weights_next = jnp.einsum(
            "eif,ecfk->ick", paired, mixing, preferred_element_type=jnp.float32
        ).reshape(row_count, width)
        offsets_next = jnp.take(offsets_now, rotation, axis=1)
        return (weights_next, offsets_next)

    current, offsets = lax.fori_loop(0, local_bits, local_level, (current, offsets))
    inner_here = lax.axis_index("gy")
    for bit_index in range(inner_bits):
        phased = turn(current, offsets, float(local_bits + bit_index + 1))
        partner = partner_2(phased, "gy", bit_index)
        child_bit = inner_here >> bit_index & 1
        current = merge_pair(phased, partner, mixing, child_bit)
    first_outer = local_bits + inner_bits
    outer_here = lax.axis_index("gx")
    for bit_index in range(outer_bits):
        phased = turn(current, offsets, float(first_outer + bit_index + 1))
        partner = partner_2(phased, "gx", bit_index)
        child_bit = outer_here >> bit_index & 1
        current = merge_pair(phased, partner, mixing, child_bit)
    finished = turn(current, offsets, float(level_count + 1))
    finished = jnp.take(finished, flipped, axis=0)
    values = jnp.dot(finished, real_form(evaluate), preferred_element_type=jnp.float32).astype(
        jnp.bfloat16
    )
    out_width = values.shape[1]
    laid_out = values.reshape(block_count, share_rows, 1, out_width)
    arrived = lax.all_to_all(laid_out, ("gx", "gy"), split_axis=0, concat_axis=2, tiled=True)
    return arrived.reshape(share_rows, block_count, out_width)


def solution(mesh):
    placed = (
        P(("gx", "gy"), None, None),
        P(("gx", "gy"), None),
        P(("gx", "gy"), None, None),
        P(),
        P(),
    )
    return jax.shard_map(
        body, mesh=mesh, in_specs=placed, out_specs=P(("gx", "gy"), None, None), check_vma=False
    )
```

profile of v0, /device:TPU:1, one launch (start us, length us, event | category | flops | bytes accessed | tf_op | source)
XLA Modules:
  0.0 1562.3 jit_solution(16800263580986790897)
XLA Ops:
  0.9 45.5 %gather_fusion.1 = s32[8192]{0:T(1024)S(1)} fusion(s32[8192]{0:T(1024)S(1)} %bitcast.102, s32[8192]{0:T(1024)S(1)} %broadcast_clamp_fusion.2), kind=kCustom, calls=%fused_computation.4 | custom fusion | bytes 98304 | tf_op jit(solution)/shard_map/jit(_take)/gather | solution.py:77
  48.8 29.5 %gather_fusion.2 = bf16[8192,128]{1,0:T(8,128)(2,1)} fusion(bf16[8192,128]{1,0:T(8,128)(2,1)S(1)} %bitcast.101, s32[8192]{0:T(1024)S(1)} %fusion.159), kind=kCustom, calls=%fused_computation.clone | custom fusion | bytes 4227072 | tf_op jit(solution)/shard_map/jit(_take)/gather | solution.py:78
  78.3 7.2 select_convert_fusion
  85.5 30.1 %gather_fusion.3 = bf16[8192,2]{1,0:T(8,128)(2,1)} fusion(bf16[2,8192]{0,1:T(8,128)(2,1)} %bitcast.108, s32[8192]{0:T(1024)S(1)} %broadcast_clamp_fusion.1), kind=kCustom, calls=%fused_computation.3.clone | custom fusion | bytes 98304 | tf_op jit(solution)/shard_map/jit(_take)/gather | solution.py:79
  121.5 963.6 %while.19 = (s32[]{:T(128)}, f32[8192,128]{1,0:T(8,128)}, bf16[2,8192]{0,1:T(8,128)(2,1)S(1)}, bf16[2,2,128,128]{3,2,0,1:T(8,128)(2,1)S(1)}, s32[]{:T(128)}) while((s32[]{:T(128)}, f32[8192,128]{1,0:T(8,128)}, bf16[2,8192]{0,1:T(8,128)(2,1)S(1)}, bf16[2,2,128,128]{3,2,0,1:T(8,128)(2,1)S(1)}, s32[]{:T(128)}) %tuple.62), condition=%wide.region_1.0_spmd.clone, body=%wide.region_0.3_spmd.clone.sunk | while | flops 547700736 | bytes 21481640 | solution.py:93
  124.2 19.1 %subtract_convert_fusion.10 = (bf16[8192,64]{1,0:T(8,128)(2,1)S(1)}, bf16[8192,64]{1,0:T(8,128)(2,1)S(1)}) fusion(f32[8192,128]{1,0:T(8,128)} %get-tuple-element.243, f32[]{:T(128)S(6)} %convert_element_type.131, f32[64]{0:T(128)S(1)} %mul.1817, f32[8192]{0:T(1024)S(1)} %get-tuple-element.233, f32[64]{0:T(128)S(1)} %mul.1818, ...), kind=kLoop, calls=%fused_computation.10.clone.1 | loop fusion | flops 6291456 | bytes 6357508 | tf_op jit(solution)/shard_map/convert.5
  144.5 16.2 %copy.38 = f32[4096,2,128]{2,1,0:T(2,128)} copy(f32[4096,2,128]{2,0,1:T(8,128)S(1)} %convolution_bitcast_fusion.2) | data formatting | bytes 8388608 | tf_op jit(solution)/shard_map/while/body/eval_jaxpr/eif,ecfk->ick/dot_general | solution.py:87
  160.7 29.5 %gather_fusion = bf16[8192,2]{1,0:T(8,128)(2,1)} fusion(bf16[2,8192]{0,1:T(8,128)(2,1)S(1)} %get-tuple-element.244, s32[8192]{0:T(1024)S(1)} %broadcast_clamp_fusion.4), kind=kCustom, calls=%fused_computation.1.clone.clone.1 | custom fusion | bytes 98304 | tf_op jit(solution)/shard_map/while/body/eval_jaxpr/jit(_take)/gather | solution.py:90
  198.3 19.1 %subtract_convert_fusion.10 = (bf16[8192,64]{1,0:T(8,128)(2,1)S(1)}, bf16[8192,64]{1,0:T(8,128)(2,1)S(1)}) fusion(f32[8192,128]{1,0:T(8,128)} %get-tuple-element.243, f32[]{:T(128)S(6)} %convert_element_type.131, f32[64]{0:T(128)S(1)} %mul.1817, f32[8192]{0:T(1024)S(1)} %get-tuple-element.233, f32[64]{0:T(128)S(1)} %mul.1818, ...), kind=kLoop, calls=%fused_computation.10.clone.1 | loop fusion | flops 6291456 | bytes 6357508 | tf_op jit(solution)/shard_map/convert.5
  218.6 16.2 %copy.38 = f32[4096,2,128]{2,1,0:T(2,128)} copy(f32[4096,2,128]{2,0,1:T(8,128)S(1)} %convolution_bitcast_fusion.2) | data formatting | bytes 8388608 | tf_op jit(solution)/shard_map/while/body/eval_jaxpr/eif,ecfk->ick/dot_general | solution.py:87
  234.8 29.5 %gather_fusion = bf16[8192,2]{1,0:T(8,128)(2,1)} fusion(bf16[2,8192]{0,1:T(8,128)(2,1)S(1)} %get-tuple-element.244, s32[8192]{0:T(1024)S(1)} %broadcast_clamp_fusion.4), kind=kCustom, calls=%fused_computation.1.clone.clone.1 | custom fusion | bytes 98304 | tf_op jit(solution)/shard_map/while/body/eval_jaxpr/jit(_take)/gather | solution.py:90
  272.4 19.1 %subtract_convert_fusion.10 = (bf16[8192,64]{1,0:T(8,128)(2,1)S(1)}, bf16[8192,64]{1,0:T(8,128)(2,1)S(1)}) fusion(f32[8192,128]{1,0:T(8,128)} %get-tuple-element.243, f32[]{:T(128)S(6)} %convert_element_type.131, f32[64]{0:T(128)S(1)} %mul.1817, f32[8192]{0:T(1024)S(1)} %get-tuple-element.233, f32[64]{0:T(128)S(1)} %mul.1818, ...), kind=kLoop, calls=%fused_computation.10.clone.1 | loop fusion | flops 6291456 | bytes 6357508 | tf_op jit(solution)/shard_map/convert.5
  292.7 16.2 %copy.38 = f32[4096,2,128]{2,1,0:T(2,128)} copy(f32[4096,2,128]{2,0,1:T(8,128)S(1)} %convolution_bitcast_fusion.2) | data formatting | bytes 8388608 | tf_op jit(solution)/shard_map/while/body/eval_jaxpr/eif,ecfk->ick/dot_general | solution.py:87
  308.9 29.5 %gather_fusion = bf16[8192,2]{1,0:T(8,128)(2,1)} fusion(bf16[2,8192]{0,1:T(8,128)(2,1)S(1)} %get-tuple-element.244, s32[8192]{0:T(1024)S(1)} %broadcast_clamp_fusion.4), kind=kCustom, calls=%fused_computation.1.clone.clone.1 | custom fusion | bytes 98304 | tf_op jit(solution)/shard_map/while/body/eval_jaxpr/jit(_take)/gather | solution.py:90
  346.5 19.1 %subtract_convert_fusion.10 = (bf16[8192,64]{1,0:T(8,128)(2,1)S(1)}, bf16[8192,64]{1,0:T(8,128)(2,1)S(1)}) fusion(f32[8192,128]{1,0:T(8,128)} %get-tuple-element.243, f32[]{:T(128)S(6)} %convert_element_type.131, f32[64]{0:T(128)S(1)} %mul.1817, f32[8192]{0:T(1024)S(1)} %get-tuple-element.233, f32[64]{0:T(128)S(1)} %mul.1818, ...), kind=kLoop, calls=%fused_computation.10.clone.1 | loop fusion | flops 6291456 | bytes 6357508 | tf_op jit(solution)/shard_map/convert.5
  366.8 16.2 %copy.38 = f32[4096,2,128]{2,1,0:T(2,128)} copy(f32[4096,2,128]{2,0,1:T(8,128)S(1)} %convolution_bitcast_fusion.2) | data formatting | bytes 8388608 | tf_op jit(solution)/shard_map/while/body/eval_jaxpr/eif,ecfk->ick/dot_general | solution.py:87
  383.0 29.5 %gather_fusion = bf16[8192,2]{1,0:T(8,128)(2,1)} fusion(bf16[2,8192]{0,1:T(8,128)(2,1)S(1)} %get-tuple-element.244, s32[8192]{0:T(1024)S(1)} %broadcast_clamp_fusion.4), kind=kCustom, calls=%fused_computation.1.clone.clone.1 | custom fusion | bytes 98304 | tf_op jit(solution)/shard_map/while/body/eval_jaxpr/jit(_take)/gather | solution.py:90
  420.6 19.1 %subtract_convert_fusion.10 = (bf16[8192,64]{1,0:T(8,128)(2,1)S(1)}, bf16[8192,64]{1,0:T(8,128)(2,1)S(1)}) fusion(f32[8192,128]{1,0:T(8,128)} %get-tuple-element.243, f32[]{:T(128)S(6)} %convert_element_type.131, f32[64]{0:T(128)S(1)} %mul.1817, f32[8192]{0:T(1024)S(1)} %get-tuple-element.233, f32[64]{0:T(128)S(1)} %mul.1818, ...), kind=kLoop, calls=%fused_computation.10.clone.1 | loop fusion | flops 6291456 | bytes 6357508 | tf_op jit(solution)/shard_map/convert.5
  440.9 16.2 %copy.38 = f32[4096,2,128]{2,1,0:T(2,128)} copy(f32[4096,2,128]{2,0,1:T(8,128)S(1)} %convolution_bitcast_fusion.2) | data formatting | bytes 8388608 | tf_op jit(solution)/shard_map/while/body/eval_jaxpr/eif,ecfk->ick/dot_general | solution.py:87
  457.1 29.5 %gather_fusion = bf16[8192,2]{1,0:T(8,128)(2,1)} fusion(bf16[2,8192]{0,1:T(8,128)(2,1)S(1)} %get-tuple-element.244, s32[8192]{0:T(1024)S(1)} %broadcast_clamp_fusion.4), kind=kCustom, calls=%fused_computation.1.clone.clone.1 | custom fusion | bytes 98304 | tf_op jit(solution)/shard_map/while/body/eval_jaxpr/jit(_take)/gather | solution.py:90
  494.6 19.1 %subtract_convert_fusion.10 = (bf16[8192,64]{1,0:T(8,128)(2,1)S(1)}, bf16[8192,64]{1,0:T(8,128)(2,1)S(1)}) fusion(f32[8192,128]{1,0:T(8,128)} %get-tuple-element.243, f32[]{:T(128)S(6)} %convert_element_type.131, f32[64]{0:T(128)S(1)} %mul.1817, f32[8192]{0:T(1024)S(1)} %get-tuple-element.233, f32[64]{0:T(128)S(1)} %mul.1818, ...), kind=kLoop, calls=%fused_computation.10.clone.1 | loop fusion | flops 6291456 | bytes 6357508 | tf_op jit(solution)/shard_map/convert.5
  515.0 16.2 %copy.38 = f32[4096,2,128]{2,1,0:T(2,128)} copy(f32[4096,2,128]{2,0,1:T(8,128)S(1)} %convolution_bitcast_fusion.2) | data formatting | bytes 8388608 | tf_op jit(solution)/shard_map/while/body/eval_jaxpr/eif,ecfk->ick/dot_general | solution.py:87
  531.2 29.5 %gather_fusion = bf16[8192,2]{1,0:T(8,128)(2,1)} fusion(bf16[2,8192]{0,1:T(8,128)(2,1)S(1)} %get-tuple-element.244, s32[8192]{0:T(1024)S(1)} %broadcast_clamp_fusion.4), kind=kCustom, calls=%fused_computation.1.clone.clone.1 | custom fusion | bytes 98304 | tf_op jit(solution)/shard_map/while/body/eval_jaxpr/jit(_take)/gather | solution.py:90
  568.7 19.1 %subtract_convert_fusion.10 = (bf16[8192,64]{1,0:T(8,128)(2,1)S(1)}, bf16[8192,64]{1,0:T(8,128)(2,1)S(1)}) fusion(f32[8192,128]{1,0:T(8,128)} %get-tuple-element.243, f32[]{:T(128)S(6)} %convert_element_type.131, f32[64]{0:T(128)S(1)} %mul.1817, f32[8192]{0:T(1024)S(1)} %get-tuple-element.233, f32[64]{0:T(128)S(1)} %mul.1818, ...), kind=kLoop, calls=%fused_computation.10.clone.1 | loop fusion | flops 6291456 | bytes 6357508 | tf_op jit(solution)/shard_map/convert.5
  589.0 16.2 %copy.38 = f32[4096,2,128]{2,1,0:T(2,128)} copy(f32[4096,2,128]{2,0,1:T(8,128)S(1)} %convolution_bitcast_fusion.2) | data formatting | bytes 8388608 | tf_op jit(solution)/shard_map/while/body/eval_jaxpr/eif,ecfk->ick/dot_general | solution.py:87
  605.2 29.5 %gather_fusion = bf16[8192,2]{1,0:T(8,128)(2,1)} fusion(bf16[2,8192]{0,1:T(8,128)(2,1)S(1)} %get-tuple-element.244, s32[8192]{0:T(1024)S(1)} %broadcast_clamp_fusion.4), kind=kCustom, calls=%fused_computation.1.clone.clone.1 | custom fusion | bytes 98304 | tf_op jit(solution)/shard_map/while/body/eval_jaxpr/jit(_take)/gather | solution.py:90
  634.8 5.8 select_bitcast_fusion.3
  642.8 19.1 %subtract_convert_fusion.10 = (bf16[8192,64]{1,0:T(8,128)(2,1)S(1)}, bf16[8192,64]{1,0:T(8,128)(2,1)S(1)}) fusion(f32[8192,128]{1,0:T(8,128)} %get-tuple-element.243, f32[]{:T(128)S(6)} %convert_element_type.131, f32[64]{0:T(128)S(1)} %mul.1817, f32[8192]{0:T(1024)S(1)} %get-tuple-element.233, f32[64]{0:T(128)S(1)} %mul.1818, ...), kind=kLoop, calls=%fused_computation.10.clone.1 | loop fusion | flops 6291456 | bytes 6357508 | tf_op jit(solution)/shard_map/convert.5
  663.1 16.2 %copy.38 = f32[4096,2,128]{2,1,0:T(2,128)} copy(f32[4096,2,128]{2,0,1:T(8,128)S(1)} %convolution_bitcast_fusion.2) | data formatting | bytes 8388608 | tf_op jit(solution)/shard_map/while/body/eval_jaxpr/eif,ecfk->ick/dot_general | solution.py:87
  679.3 29.5 %gather_fusion = bf16[8192,2]{1,0:T(8,128)(2,1)} fusion(bf16[2,8192]{0,1:T(8,128)(2,1)S(1)} %get-tuple-element.244, s32[8192]{0:T(1024)S(1)} %broadcast_clamp_fusion.4), kind=kCustom, calls=%fused_computation.1.clone.clone.1 | custom fusion | bytes 98304 | tf_op jit(solution)/shard_map/while/body/eval_jaxpr/jit(_take)/gather | solution.py:90
  708.8 5.8 select_bitcast_fusion.3
  716.9 19.1 %subtract_convert_fusion.10 = (bf16[8192,64]{1,0:T(8,128)(2,1)S(1)}, bf16[8192,64]{1,0:T(8,128)(2,1)S(1)}) fusion(f32[8192,128]{1,0:T(8,128)} %get-tuple-element.243, f32[]{:T(128)S(6)} %convert_element_type.131, f32[64]{0:T(128)S(1)} %mul.1817, f32[8192]{0:T(1024)S(1)} %get-tuple-element.233, f32[64]{0:T(128)S(1)} %mul.1818, ...), kind=kLoop, calls=%fused_computation.10.clone.1 | loop fusion | flops 6291456 | bytes 6357508 | tf_op jit(solution)/shard_map/convert.5
  737.2 16.2 %copy.38 = f32[4096,2,128]{2,1,0:T(2,128)} copy(f32[4096,2,128]{2,0,1:T(8,128)S(1)} %convolution_bitcast_fusion.2) | data formatting | bytes 8388608 | tf_op jit(solution)/shard_map/while/body/eval_jaxpr/eif,ecfk->ick/dot_general | solution.py:87
  753.4 29.5 %gather_fusion = bf16[8192,2]{1,0:T(8,128)(2,1)} fusion(bf16[2,8192]{0,1:T(8,128)(2,1)S(1)} %get-tuple-element.244, s32[8192]{0:T(1024)S(1)} %broadcast_clamp_fusion.4), kind=kCustom, calls=%fused_computation.1.clone.clone.1 | custom fusion | bytes 98304 | tf_op jit(solution)/shard_map/while/body/eval_jaxpr/jit(_take)/gather | solution.py:90
  782.9 5.8 select_bitcast_fusion.3
  791.0 19.1 %subtract_convert_fusion.10 = (bf16[8192,64]{1,0:T(8,128)(2,1)S(1)}, bf16[8192,64]{1,0:T(8,128)(2,1)S(1)}) fusion(f32[8192,128]{1,0:T(8,128)} %get-tuple-element.243, f32[]{:T(128)S(6)} %convert_element_type.131, f32[64]{0:T(128)S(1)} %mul.1817, f32[8192]{0:T(1024)S(1)} %get-tuple-element.233, f32[64]{0:T(128)S(1)} %mul.1818, ...), kind=kLoop, calls=%fused_computation.10.clone.1 | loop fusion | flops 6291456 | bytes 6357508 | tf_op jit(solution)/shard_map/convert.5
  811.3 16.2 %copy.38 = f32[4096,2,128]{2,1,0:T(2,128)} copy(f32[4096,2,128]{2,0,1:T(8,128)S(1)} %convolution_bitcast_fusion.2) | data formatting | bytes 8388608 | tf_op jit(solution)/shard_map/while/body/eval_jaxpr/eif,ecfk->ick/dot_general | solution.py:87
  827.5 29.5 %gather_fusion = bf16[8192,2]{1,0:T(8,128)(2,1)} fusion(bf16[2,8192]{0,1:T(8,128)(2,1)S(1)} %get-tuple-element.244, s32[8192]{0:T(1024)S(1)} %broadcast_clamp_fusion.4), kind=kCustom, calls=%fused_computation.1.clone.clone.1 | custom fusion | bytes 98304 | tf_op jit(solution)/shard_map/while/body/eval_jaxpr/jit(_take)/gather | solution.py:90
  857.0 5.8 select_bitcast_fusion.3
  865.1 19.1 %subtract_convert_fusion.10 = (bf16[8192,64]{1,0:T(8,128)(2,1)S(1)}, bf16[8192,64]{1,0:T(8,128)(2,1)S(1)}) fusion(f32[8192,128]{1,0:T(8,128)} %get-tuple-element.243, f32[]{:T(128)S(6)} %convert_element_type.131, f32[64]{0:T(128)S(1)} %mul.1817, f32[8192]{0:T(1024)S(1)} %get-tuple-element.233, f32[64]{0:T(128)S(1)} %mul.1818, ...), kind=kLoop, calls=%fused_computation.10.clone.1 | loop fusion | flops 6291456 | bytes 6357508 | tf_op jit(solution)/shard_map/convert.5
  885.4 16.2 %copy.38 = f32[4096,2,128]{2,1,0:T(2,128)} copy(f32[4096,2,128]{2,0,1:T(8,128)S(1)} %convolution_bitcast_fusion.2) | data formatting | bytes 8388608 | tf_op jit(solution)/shard_map/while/body/eval_jaxpr/eif,ecfk->ick/dot_general | solution.py:87
  901.6 29.5 %gather_fusion = bf16[8192,2]{1,0:T(8,128)(2,1)} fusion(bf16[2,8192]{0,1:T(8,128)(2,1)S(1)} %get-tuple-element.244, s32[8192]{0:T(1024)S(1)} %broadcast_clamp_fusion.4), kind=kCustom, calls=%fused_computation.1.clone.clone.1 | custom fusion | bytes 98304 | tf_op jit(solution)/shard_map/while/body/eval_jaxpr/jit(_take)/gather | solution.py:90
  939.2 19.1 %subtract_convert_fusion.10 = (bf16[8192,64]{1,0:T(8,128)(2,1)S(1)}, bf16[8192,64]{1,0:T(8,128)(2,1)S(1)}) fusion(f32[8192,128]{1,0:T(8,128)} %get-tuple-element.243, f32[]{:T(128)S(6)} %convert_element_type.131, f32[64]{0:T(128)S(1)} %mul.1817, f32[8192]{0:T(1024)S(1)} %get-tuple-element.233, f32[64]{0:T(128)S(1)} %mul.1818, ...), kind=kLoop, calls=%fused_computation.10.clone.1 | loop fusion | flops 6291456 | bytes 6357508 | tf_op jit(solution)/shard_map/convert.5
  959.5 16.2 %copy.38 = f32[4096,2,128]{2,1,0:T(2,128)} copy(f32[4096,2,128]{2,0,1:T(8,128)S(1)} %convolution_bitcast_fusion.2) | data formatting | bytes 8388608 | tf_op jit(solution)/shard_map/while/body/eval_jaxpr/eif,ecfk->ick/dot_general | solution.py:87
  975.7 29.5 %gather_fusion = bf16[8192,2]{1,0:T(8,128)(2,1)} fusion(bf16[2,8192]{0,1:T(8,128)(2,1)S(1)} %get-tuple-element.244, s32[8192]{0:T(1024)S(1)} %broadcast_clamp_fusion.4), kind=kCustom, calls=%fused_computation.1.clone.clone.1 | custom fusion | bytes 98304 | tf_op jit(solution)/shard_map/while/body/eval_jaxpr/jit(_take)/gather | solution.py:90
  1013.3 19.1 %subtract_convert_fusion.10 = (bf16[8192,64]{1,0:T(8,128)(2,1)S(1)}, bf16[8192,64]{1,0:T(8,128)(2,1)S(1)}) fusion(f32[8192,128]{1,0:T(8,128)} %get-tuple-element.243, f32[]{:T(128)S(6)} %convert_element_type.131, f32[64]{0:T(128)S(1)} %mul.1817, f32[8192]{0:T(1024)S(1)} %get-tuple-element.233, f32[64]{0:T(128)S(1)} %mul.1818, ...), kind=kLoop, calls=%fused_computation.10.clone.1 | loop fusion | flops 6291456 | bytes 6357508 | tf_op jit(solution)/shard_map/convert.5
  1033.6 16.2 %copy.38 = f32[4096,2,128]{2,1,0:T(2,128)} copy(f32[4096,2,128]{2,0,1:T(8,128)S(1)} %convolution_bitcast_fusion.2) | data formatting | bytes 8388608 | tf_op jit(solution)/shard_map/while/body/eval_jaxpr/eif,ecfk->ick/dot_general | solution.py:87
  1049.8 29.5 %gather_fusion = bf16[8192,2]{1,0:T(8,128)(2,1)} fusion(bf16[2,8192]{0,1:T(8,128)(2,1)S(1)} %get-tuple-element.244, s32[8192]{0:T(1024)S(1)} %broadcast_clamp_fusion.4), kind=kCustom, calls=%fused_computation.1.clone.clone.1 | custom fusion | bytes 98304 | tf_op jit(solution)/shard_map/while/body/eval_jaxpr/jit(_take)/gather | solution.py:90
  1093.0 9.9 subtract_convert_fusion.8
  1107.6 44.9 %collective-permute-done = bf16[8192,128]{0,1:T(8,128)(2,1)} collective-permute-done((bf16[8192,128]{0,1:T(8,128)(2,1)}, bf16[8192,128]{0,1:T(8,128)(2,1)}, u32[]{:S(2)}, u32[]{:S(2)}) %collective-permute-start) | collective-permute-done | bytes 2097184 | tf_op jit(solution)/shard_map/ppermute | solution.py:16
  1154.9 8.3 subtract_convert_fusion.7
  1168.7 44.0 %collective-permute-done.1 = bf16[8192,128]{0,1:T(8,128)(2,1)} collective-permute-done((bf16[8192,128]{0,1:T(8,128)(2,1)}, bf16[8192,128]{0,1:T(8,128)(2,1)}, u32[]{:S(2)}, u32[]{:S(2)}) %collective-permute-start.1) | collective-permute-done | bytes 2097184 | tf_op jit(solution)/shard_map/ppermute | solution.py:16
  1215.0 8.3 subtract_convert_fusion.6
  1226.9 43.2 %collective-permute-done.2 = bf16[8192,128]{0,1:T(8,128)(2,1)} collective-permute-done((bf16[8192,128]{0,1:T(8,128)(2,1)}, bf16[8192,128]{0,1:T(8,128)(2,1)}, u32[]{:S(2)}, u32[]{:S(2)}) %collective-permute-start.2) | collective-permute-done | bytes 2097184 | tf_op jit(solution)/shard_map/ppermute | solution.py:16
  1272.5 8.6 subtract_convert_fusion.5
  1286.3 42.1 %collective-permute-done.3 = bf16[8192,128]{0,1:T(8,128)(2,1)} collective-permute-done((bf16[8192,128]{0,1:T(8,128)(2,1)}, bf16[8192,128]{0,1:T(8,128)(2,1)}, u32[]{:S(2)}, u32[]{:S(2)}) %collective-permute-start.3) | collective-permute-done | bytes 2097184 | tf_op jit(solution)/shard_map/ppermute | solution.py:16
  1330.8 8.3 subtract_convert_fusion.4
  1351.3 8.3 subtract_convert_fusion.3
  1363.1 45.2 %collective-permute-done.5 = bf16[8192,128]{0,1:T(8,128)(2,1)} collective-permute-done((bf16[8192,128]{0,1:T(8,128)(2,1)}, bf16[8192,128]{0,1:T(8,128)(2,1)}, u32[]{:S(2)}, u32[]{:S(2)}) %collective-permute-start.5) | collective-permute-done | bytes 2097184 | tf_op jit(solution)/shard_map/ppermute | solution.py:16
  1410.7 8.6 subtract_convert_fusion.2
  1424.3 44.2 %collective-permute-done.6 = bf16[8192,128]{0,1:T(8,128)(2,1)} collective-permute-done((bf16[8192,128]{0,1:T(8,128)(2,1)}, bf16[8192,128]{0,1:T(8,128)(2,1)}, u32[]{:S(2)}, u32[]{:S(2)}) %collective-permute-start.6) | collective-permute-done | bytes 2097184 | tf_op jit(solution)/shard_map/ppermute | solution.py:16
  1471.0 8.3 subtract_convert_fusion.1
  1484.0 29.5 %gather_fusion.4 = bf16[8192,128]{1,0:T(8,128)(2,1)} fusion(bf16[8192,128]{1,0:T(8,128)(2,1)S(1)} %copy.27, s32[8192]{0:T(1024)S(1)} %broadcast_clamp_fusion.1), kind=kCustom, calls=%fused_computation.2.clone | custom fusion | bytes 4227072 | tf_op jit(solution)/shard_map/jit(_take)/gather | solution.py:108
  1519.0 40.2 %all_to_all.15 = bf16[128,64,1,128]{3,1,2,0:T(8,128)(2,1)S(1)} all-to-all(bf16[128,64,1,128]{3,1,2,0:T(8,128)(2,1)S(1)} %bitcast.106), channel_id=1, replica_groups=mesh['gx'=8,'gy'=16] {'gx','gy'}, dimensions={0} | all-to-all | bytes 4194304 | tf_op jit(solution)/shard_map/all_to_all | solution.py:114
  (192 shorter events, 181.4 us)
Async XLA Ops:
  0.0 48.8 %copy-start = (bf16[1,8192,128]{2,1,0:T(8,128)(2,1)S(1)}, bf16[1,8192,128]{2,1,0:T(8,128)(2,1)}, u32[]{:S(2)}) copy-start(bf16[1,8192,128]{2,1,0:T(8,128)(2,1)} %param.11) | copy-start | bytes 6291460
  0.0 0.9 copy-start.2
  0.9 45.9 %copy-start.3 = (bf16[2,2,2,64,64]{4,3,2,1,0:T(8,128)(2,1)S(1)}, bf16[2,2,2,64,64]{4,3,2,1,0:T(8,128)(2,1)}, u32[]{:S(2)}) copy-start(bf16[2,2,2,64,64]{4,3,2,1,0:T(8,128)(2,1)} %param.14) | copy-start | bytes 196612
  0.9 46.0 %copy-start.5 = (bf16[1,2,8192]{2,1,0:T(2,128)(2,1)S(1)}, bf16[1,2,8192]{2,1,0:T(2,128)(2,1)}, u32[]{:S(2)}) copy-start(bf16[1,2,8192]{2,1,0:T(2,128)(2,1)} %param.13) | copy-start | bytes 98308
  1104.4 48.1 %collective-permute-start = (bf16[8192,128]{0,1:T(8,128)(2,1)}, bf16[8192,128]{0,1:T(8,128)(2,1)}, u32[]{:S(2)}, u32[]{:S(2)}) collective-permute-start(bf16[8192,128]{0,1:T(8,128)(2,1)} %pad_maximum_fusion), channel_id=1, source_target_pairs={{0,1},{1,0},{2,3},{3,2},{4,5},{5,4},{6,7},{7,6},{8,9},{9,8},{10,11... | collective-permute-start | bytes 6291464 | tf_op jit(solution)/shard_map/ppermute | solution.py:16
  1164.8 47.8 %collective-permute-start.1 = (bf16[8192,128]{0,1:T(8,128)(2,1)}, bf16[8192,128]{0,1:T(8,128)(2,1)}, u32[]{:S(2)}, u32[]{:S(2)}) collective-permute-start(bf16[8192,128]{0,1:T(8,128)(2,1)} %pad_maximum_fusion.1), channel_id=1, source_target_pairs={{0,2},{2,0},{1,3},{3,1},{4,6},{6,4},{5,7},{7,5},{8,10},{10,8},{9,1... | collective-permute-start | bytes 6291464 | tf_op jit(solution)/shard_map/ppermute | solution.py:16
  1224.9 45.3 %collective-permute-start.2 = (bf16[8192,128]{0,1:T(8,128)(2,1)}, bf16[8192,128]{0,1:T(8,128)(2,1)}, u32[]{:S(2)}, u32[]{:S(2)}) collective-permute-start(bf16[8192,128]{0,1:T(8,128)(2,1)} %pad_maximum_fusion.2), channel_id=1, source_target_pairs={{0,4},{4,0},{1,5},{5,1},{2,6},{6,2},{3,7},{7,3},{8,12},{12,8},{9,1... | collective-permute-start | bytes 6291464 | tf_op jit(solution)/shard_map/ppermute | solution.py:16
  1282.6 45.8 %collective-permute-start.3 = (bf16[8192,128]{0,1:T(8,128)(2,1)}, bf16[8192,128]{0,1:T(8,128)(2,1)}, u32[]{:S(2)}, u32[]{:S(2)}) collective-permute-start(bf16[8192,128]{0,1:T(8,128)(2,1)} %pad_maximum_fusion.3), channel_id=1, source_target_pairs={{0,8},{8,0},{1,9},{9,1},{2,10},{10,2},{3,11},{11,3},{4,12},{12,4},... | collective-permute-start | bytes 6291464 | tf_op jit(solution)/shard_map/ppermute | solution.py:16
  1340.7 8.2 collective-permute-start.4
  1361.1 47.2 %collective-permute-start.5 = (bf16[8192,128]{0,1:T(8,128)(2,1)}, bf16[8192,128]{0,1:T(8,128)(2,1)}, u32[]{:S(2)}, u32[]{:S(2)}) collective-permute-start(bf16[8192,128]{0,1:T(8,128)(2,1)} %pad_maximum_fusion.5), channel_id=1, source_target_pairs={{0,32},{32,0},{16,48},{48,16},{64,96},{96,64},{80,112},{112,80},{1... | collective-permute-start | bytes 6291464 | tf_op jit(solution)/shard_map/ppermute | solution.py:16
  1419.3 4.3 copy-start.4
  1420.8 47.7 %collective-permute-start.6 = (bf16[8192,128]{0,1:T(8,128)(2,1)}, bf16[8192,128]{0,1:T(8,128)(2,1)}, u32[]{:S(2)}, u32[]{:S(2)}) collective-permute-start(bf16[8192,128]{0,1:T(8,128)(2,1)} %pad_maximum_fusion.6), channel_id=1, source_target_pairs={{0,64},{64,0},{16,80},{80,16},{32,96},{96,32},{48,112},{112,48},{1... | collective-permute-start | bytes 6291464 | tf_op jit(solution)/shard_map/ppermute | solution.py:16
  1559.2 2.7 copy-start.1
where the time goes:
time: 1570 us; the launch traced here: 1560 us
  local copies, waits for them, and re-layouts  745 us (47%)
  other arithmetic  446 us (28%)
  waiting for transfers between devices  267 us (17%)
  matrix products  43.7 us (3%)
  blocking collectives  40.2 us (3%)
  starting transfers between devices  17.8 us (1%)
    gather x13, local copies, waits for them, and re-layouts, local_level(): offsets_next = jnp.take(offsets_now, rotation, axis=1)  383 us
    another operation x21, other arithmetic  316 us
    ppermute x7, waiting for transfers between devices, partner_2(): return lax.ppermute(block, axis, route)  267 us
    dot_general x13, local copies, waits for them, and re-layouts, local_level(): jnp.einsum('eif,ecfk->ick', paired, mixing, preferred_element_type=jnp.fl...  210 us
    select_n x13, other arithmetic, local_level(): offsets_next = jnp.take(offsets_now, rotation, axis=1)  75.8 us
    gather x1, local copies, waits for them, and re-layouts, body(): slots = jnp.take(leaf_slot[0], flipped, axis=0)  45.5 us
    all_to_all x1, blocking collectives, body(): lax.all_to_all(laid_out, ('gx', 'gy'), split_axis=0, concat_axis=2, tiled...  40.2 us
  transfers between devices with their start and end apart: 7, of which 7 were waited for; matrix products, arithmetic and copies ran while one was open for 0% of the time, Pallas kernels for 0%

commit v1 on v0

v1 whole, which is shorter than its diff:
```python
import functools
import math

import jax
import jax.numpy as jnp
import numpy as np
from jax import lax
from jax.experimental import pallas as pl
from jax.experimental.pallas import tpu as pltpu
from jax.sharding import PartitionSpec as P

MESH = pl.DeviceIdType.MESH
F32 = jnp.float32
BF16 = jnp.bfloat16
TURN = 2.0 * math.pi
SIN_TERMS = None


def sine_terms():
    k = np.arange(400)
    w = 0.125 * (1 + np.cos(np.pi * (k + 0.5) / 400))
    v = w * w
    basis = np.stack([w * v**j for j in range(5)], axis=1)
    weight = 1.0 / np.sqrt(np.sin(TURN * w) + 1e-3)
    coef = np.linalg.lstsq(basis * weight[:, None], np.sin(TURN * w) * weight, rcond=None)[0]
    return [float(c) for c in coef]


SIN_TERMS = sine_terms()
TILES = 8
ROLL16 = True
PARTS = ("gather", "z1", "p1", "z2", "p2", "comm", "z3", "p3")


def cosine_turns(x):
    x = x - jnp.round(x)
    w = 0.25 - jnp.abs(x)
    v = w * w
    r = SIN_TERMS[4] * v + SIN_TERMS[3]
    r = r * v + SIN_TERMS[2]
    r = r * v + SIN_TERMS[1]
    r = r * v + SIN_TERMS[0]
    return r * w


def swap(tile):
    if ROLL16:
        return pltpu.roll(tile, 64, 1)
    return pltpu.roll(tile.astype(F32), 64, 1).astype(BF16)


def kernel(parts, ch_ref, slot_ref, off_ref, lag_ref, ev_ref, nodes_ref, out_ref,
           cf, g, zt, x, send, recv, ab, ro, at, w, ev, ob, o32, ssem, rsem, offs, offr, osem):
    gx, gy = lax.axis_index("gx"), lax.axis_index("gy")
    me = gx * 16 + gy
    comm = "comm" in parts
    if comm:
        bar = pltpu.get_barrier_semaphore()

        @pl.loop(1, 128)
        def _(k):
            dst = (me + k) & 127
            pl.semaphore_signal(bar, inc=1, device_id=(dst >> 4, dst & 15), device_id_type=MESH)

    for e in range(2):
        for c in range(2):
            re = lag_ref[e, c, 0].astype(F32)
            im = lag_ref[e, c, 1].astype(F32)
            w[pl.ds(e * 128, 64), pl.ds(c * 128, 128)] = jnp.concatenate([re, im], axis=1).astype(BF16)
            w[pl.ds(e * 128 + 64, 64), pl.ds(c * 128, 128)] = jnp.concatenate([-im, re], axis=1).astype(BF16)
    re = ev_ref[0].astype(F32)
    im = ev_ref[1].astype(F32)
    ev[pl.ds(0, 64), :] = jnp.concatenate([re, im], axis=1).astype(BF16)
    ev[pl.ds(64, 64), :] = jnp.concatenate([-im, re], axis=1).astype(BF16)

    for m in range(64):
        ab[m] = off_ref[0, :, pl.ds(m * 128, 128)].astype(F32)
    for k in range(2):
        rows = ab[:, k, :]
        at[k] = jnp.concatenate([rows, rows], axis=0).T
        at[2 + k, pl.ds(0, 64)] = rows

    lane = lax.broadcasted_iota(jnp.int32, (16, 128), 1)
    low = lane < 64
    ui = nodes_ref[0:1, :]
    uj = nodes_ref[1:2, :]
    quarter = jnp.where(low, 0.0, -0.25).astype(F32)

    def column(ref, k, row, j):
        return jnp.broadcast_to(pltpu.roll(ref[k, pl.ds(row, 16), :], (128 - j) & 127, 1)[:, 0:1], (16, 128))

    def many_phases(total, place, offset_of, first, count):
        @pl.loop(0, total, step=TILES)
        def _(j):
            spots = [place(j + u) for u in range(TILES)]
            state = []
            for u in range(TILES):
                a, b = offset_of(j + u)
                tau = a * ui + b * uj
                if first == 1:
                    now = cosine_turns(tau + quarter)
                    twice = 2.0 * jnp.where(low, now, pltpu.roll(now, 64, 1))
                    before = jnp.where(low, 1.0, 0.0).astype(F32)
                else:
                    twice = 2.0 * cosine_turns(tau)
                    now = cosine_turns(tau * float(first) + quarter)
                    before = cosine_turns(tau * float(first - 1) + quarter)
                state.append((now, before, twice))
            for l in range(count):
                for u in range(TILES):
                    now, before, twice = state[u]
                    i, q = spots[u]
                    zb = now.astype(BF16)
                    rb = swap(zb)
                    zt[i, l, q, :, pl.ds(0, 128)] = jnp.where(low, zb, rb)
                    zt[i, l, q, :, pl.ds(128, 128)] = jnp.where(low, -rb, zb)
                    if l + 1 < count:
                        state[u] = (twice * now - before, now, twice)

    def turned(tile, i, l, q):
        return tile * zt[i, l, q, :, pl.ds(0, 128)] + swap(tile) * zt[i, l, q, :, pl.ds(128, 128)]

    def level(i, l, bit, load, save, per=32):
        for blk in range(64 // per):
            rows = []
            idx = []
            for p in range(blk * per, (blk + 1) * per):
                q0 = ((p >> bit) << (bit + 1)) | (p & ((1 << bit) - 1))
                q1 = q0 | (1 << bit)
                idx.append((q0, q1))
                rows.append(jnp.concatenate([turned(load(q0), i, l, q0), turned(load(q1), i, l, q1)], axis=1))
            o = jnp.dot(jnp.concatenate(rows, axis=0), w[...], preferred_element_type=F32)
            for j, (q0, q1) in enumerate(idx):
                save(q0, o[16 * j:16 * j + 16, 0:128])
                save(q1, o[16 * j:16 * j + 16, 128:256])

    def load_x(q):
        return x[q]

    def save_x(q, v):
        x[q] = v.astype(BF16)

    @pl.loop(0, 8)
    def _(j):
        cf[pl.ds(j * 1024, 1024), :] = ch_ref[0, pl.ds(j * 1024, 1024), :].astype(F32)

    @pl.loop(0, 4)
    def _(i):
        @pl.loop(0, 128)
        def _(q):
            if "gather" in parts:
                base = i * 2048 + q
                for s in range(16):
                    slot = slot_ref[0, base + s * 128]
                    g[i, q, pl.ds(s, 1), :] = cf[pl.ds(slot, 1), :]

        if "z1" in parts:
            many_phases(128, lambda j: (i, j), lambda j: (column(at, 2, i * 16, j), column(at, 3, i * 16, j)), 1, 7)

    if "p1" in parts:
        @pl.loop(0, 4)
        def _(i):
            for l in range(7):
                load = load_x if l > 0 else (lambda q: g[i, q].astype(BF16))
                if l < 6:
                    save = save_x
                else:
                    def save(q, v):
                        c, t, hi = (q >> 4) & 3, q & 15, q >> 6
                        cf[pl.ds(((c * 64 + 16 * i) * 2 + hi) * 16 + t, 16, stride=32), :] = v
                level(i, l, l, load, save)

    if comm:
        pl.semaphore_wait(bar, 127)

        @pl.loop(1, 128)
        def _(k):
            dst = (me + k) & 127
            pltpu.make_async_remote_copy(src_ref=ab.at[dst >> 1], dst_ref=ro.at[me], send_sem=offs.at[0],
                                         recv_sem=offr.at[0], device_id=(dst >> 4, dst & 15), device_id_type=MESH).start()
        pltpu.make_async_copy(ab.at[me >> 1], ro.at[me], offr.at[0]).start()

    @pl.loop(0, 4)
    def _(c):
        if "z2" in parts:
            many_phases(128, lambda j: (0, j), lambda j: (
                column(at, 0, (j & 1) * 64 + c * 16, j >> 1), column(at, 1, (j & 1) * 64 + c * 16, j >> 1)), 8, 6)
        if "p2" in parts:
            for l in range(6):
                load = load_x if l > 0 else (lambda q: cf[pl.ds((c * 128 + q) * 16, 16), :].astype(BF16))
                if l < 5:
                    save = save_x
                else:
                    def save(q, v):
                        send[c, q] = v.astype(BF16)
                level(0, l, l + 1, load, save)
        if comm:
            @pl.loop(1, 128)
            def _(k):
                dst = (me + k) & 127
                pltpu.make_async_remote_copy(src_ref=send.at[c, dst], dst_ref=recv.at[c, me], send_sem=ssem.at[c],
                                             recv_sem=rsem.at[c], device_id=(dst >> 4, dst & 15), device_id_type=MESH).start()
            pltpu.make_async_copy(send.at[c, me], recv.at[c, me], rsem.at[c]).start()

    if comm:
        pltpu.make_async_copy(ro, ro, offr.at[0]).wait()
    for k in range(2):
        at[k] = ro[:, k, :].T
    half = (me & 1) * 64

    if "z3" in parts:
        @pl.loop(0, 4)
        def _(c):
            row = pl.multiple_of(half + c * 16, 16)
            many_phases(128, lambda j: (c, j), lambda j: (column(at, 0, row, j), column(at, 1, row, j)), 14, 8)

    @pl.loop(0, 4)
    def _(c):
        if comm:
            pltpu.make_async_copy(recv.at[c], recv.at[c], rsem.at[c]).wait()
        if "p3" in parts:
            for l in range(7):
                level(c, l, l, load_x if l > 0 else (lambda q: recv[c, q]), save_x)
            for blk in range(4):
                rows = jnp.concatenate([turned(x[q], c, 7, q) for q in range(blk * 32, blk * 32 + 32)], axis=0)
                v = jnp.dot(rows, ev[...], preferred_element_type=F32)
                for j in range(32):
                    o32[pl.ds(blk * 32 + j, 16, stride=128), :] = v[16 * j:16 * j + 16]
            for t in range(16):
                ob[c, t] = o32[pl.ds(t * 128, 128), :].astype(BF16)
        pltpu.make_async_copy(ob.at[c], out_ref.at[pl.ds(c * 16, 16)], osem.at[c]).start()

    for c in range(4):
        pltpu.make_async_copy(ob.at[c], out_ref.at[pl.ds(c * 16, 16)], osem.at[c]).wait()
    if comm:
        pltpu.make_async_copy(ro.at[pl.ds(0, 127)], ro.at[pl.ds(0, 127)], offs.at[0]).wait()
        for c in range(4):
            pltpu.make_async_copy(recv.at[c, pl.ds(0, 127)], recv.at[c, pl.ds(0, 127)], ssem.at[c]).wait()


def chebyshev_lanes():
    side = 8
    u = np.cos(math.pi * (2.0 * np.arange(side) + 1.0) / (2.0 * side))
    row = np.repeat(u, side)
    col = np.tile(u, side)
    table = np.zeros((8, 128))
    table[0] = np.concatenate([row, row]) / TURN
    table[1] = np.concatenate([col, col]) / TURN
    return table.astype(np.float32)


def body(charges, leaf_slot, node_offset, lagrange, evaluate, parts=PARTS):
    vm = pl.BlockSpec(memory_space=pltpu.VMEM)
    comm = "comm" in parts
    cp = dict(collective_id=0) if comm else {}
    return pl.pallas_call(
        functools.partial(kernel, parts),
        out_shape=jax.ShapeDtypeStruct((64, 128, 128), BF16),
        in_specs=[vm, pl.BlockSpec(memory_space=pltpu.SMEM), vm, vm, vm, vm],
        out_specs=pl.BlockSpec(memory_space=pl.ANY),
        scratch_shapes=[
            pltpu.VMEM((8192, 128), F32),
            pltpu.VMEM((4, 128, 16, 128), F32),
            pltpu.VMEM((4, 8, 128, 16, 256), BF16),
            pltpu.VMEM((128, 16, 128), BF16),
            pltpu.VMEM((4, 128, 16, 128), BF16),
            pltpu.VMEM((4, 128, 16, 128), BF16),
            pltpu.VMEM((64, 2, 128), F32),
            pltpu.VMEM((128, 2, 128), F32),
            pltpu.VMEM((4, 128, 128), F32),
            pltpu.VMEM((256, 256), BF16),
            pltpu.VMEM((128, 128), BF16),
            pltpu.VMEM((4, 16, 128, 128), BF16),
            pltpu.VMEM((2048, 128), F32),
            pltpu.SemaphoreType.DMA((4,)), pltpu.SemaphoreType.DMA((4,)),
            pltpu.SemaphoreType.DMA((1,)), pltpu.SemaphoreType.DMA((1,)), pltpu.SemaphoreType.DMA((4,)),
        ],
        compiler_params=pltpu.CompilerParams(has_side_effects=True, vmem_limit_bytes=60 << 20, **cp),
    )(charges, leaf_slot, node_offset, lagrange, evaluate, jnp.asarray(chebyshev_lanes()))


def solution(mesh, parts=PARTS):
    placed = (P(("gx", "gy"), None, None), P(("gx", "gy"), None), P(("gx", "gy"), None, None), P(), P())
    return jax.shard_map(functools.partial(body, parts=parts), mesh=mesh, in_specs=placed,
                         out_specs=P(("gx", "gy"), None, None), check_vma=False)
```

time: 1570 us -> 131 us (0.08)
  local copies, waits for them, and re-layouts: 745 us -> 3.16 us
  other arithmetic: 446 us -> 0 us
  waiting for transfers between devices: 267 us -> 0 us
  Pallas kernels: 0 us -> 128 us
  matrix products: 43.7 us -> 0 us
  blocking collectives: 40.2 us -> 0 us
  starting transfers between devices: 17.8 us -> 0 us
    gather x17 -> x0, local copies, waits for them, and re-layouts: 518 us -> none  [the longest x13 383 us: local_level(): offsets_next = jnp.take(offsets_now, rotation, axis=1)]
    another operation x21 -> x0, other arithmetic: 316 us -> none
    ppermute x7 -> x0, waiting for transfers between devices: 267 us -> none  [partner_2(): return lax.ppermute(block, axis, route)]
    dot_general x13 -> x0, local copies, waits for them, and re-layouts: 210 us -> none  [local_level(): jnp.einsum('eif,ecfk->ick', paired, mixing, preferred_element_type=jnp.fl...]
    pallas_call x0 -> x1, Pallas kernels: none -> 128 us  [body(): pl.pallas_call(functools.partial(kernel, parts), out_shape=jax.ShapeDtype...]
    select_n x15 -> x0, other arithmetic: 82 us -> none  [the longest x13 75.8 us: local_level(): offsets_next = jnp.take(offsets_now, rotation, axis=1)]
    dot_general x28 -> x0, matrix products: 43.7 us -> none  [the longest x7 16.8 us: merge_pair(): jnp.dot(partner, far_matrix, preferred_element_type=jnp.float32)]
    all_to_all x1 -> x0, blocking collectives: 40.2 us -> none  [body(): lax.all_to_all(laid_out, ('gx', 'gy'), split_axis=0, concat_axis=2, tiled...]
  transfers between devices with their start and end apart: 7 -> 0, of which waited for: 7 -> 0; matrix products, arithmetic and copies ran while one was open for 0% -> 0% of each run, Pallas kernels for 0% -> 0%
where the time goes in v1:
time: 131 us
  Pallas kernels  128 us (98%)
  local copies, waits for them, and re-layouts  3.16 us (2%)
    pallas_call x1, Pallas kernels, body(): pl.pallas_call(functools.partial(kernel, parts), out_shape=jax.ShapeDtype...  128 us
    unnamed x1, local copies, waits for them, and re-layouts  3.16 us

profile of v1, /device:TPU:1, one launch (start us, length us, event | category | flops | bytes accessed | tf_op | source)
XLA Modules:
  0.0 131.0 jit_solution(3007817942818457298)
XLA Ops:
  0.0 127.8 %shard_map.64 = bf16[64,128,128]{2,1,0:T(8,128)(2,1)} custom-call(bf16[1,8192,128]{2,1,0:T(8,128)(2,1)} %ch_ref.1, s32[1,8192]{1,0:T(1,128)} %slot_ref.1, bf16[1,2,8192]{2,1,0:T(2,128)(2,1)} %off_ref.1, bf16[2,2,2,64,64]{4,3,2,1,0:T(8,128)(2,1)} %lag_ref.1, bf16[2,64,64]{2,1,0:T(8,128)(2,1)} %ev_ref.1, f32[8,128]{1,0:T(8,128)} %constant.2.clone.nodes_ref), custom_call_target="tpu_custom_call" | custom-call | tf_op jit(solution)/shard_map/pallas_call | solution.py:256
  127.8 3.2 %copy.8 = bf16[64,128,128]{2,1,0:T(8,128)(2,1)} copy(bf16[64,128,128]{2,1,0:T(8,128)(2,1)} %shard_map.64) | data formatting | bytes 4194304

commit v2 on v1

--- a/solution.py
+++ b/solution.py
@@ -20,7 +20,7 @@
     k = np.arange(400)
     w = 0.125 * (1 + np.cos(np.pi * (k + 0.5) / 400))
     v = w * w
-    basis = np.stack([w * v**j for j in range(5)], axis=1)
+    basis = np.stack([w * v**j for j in range(4)], axis=1)
     weight = 1.0 / np.sqrt(np.sin(TURN * w) + 1e-3)
     coef = np.linalg.lstsq(basis * weight[:, None], np.sin(TURN * w) * weight, rcond=None)[0]
     return [float(c) for c in coef]
@@ -36,8 +36,7 @@
     x = x - jnp.round(x)
     w = 0.25 - jnp.abs(x)
     v = w * w
-    r = SIN_TERMS[4] * v + SIN_TERMS[3]
-    r = r * v + SIN_TERMS[2]
+    r = SIN_TERMS[3] * v + SIN_TERMS[2]
     r = r * v + SIN_TERMS[1]
     r = r * v + SIN_TERMS[0]
     return r * w
@@ -50,7 +49,7 @@
 
 
 def kernel(parts, ch_ref, slot_ref, off_ref, lag_ref, ev_ref, nodes_ref, out_ref,
-           cf, g, zt, x, send, recv, ab, ro, at, w, ev, ob, o32, ssem, rsem, offs, offr, osem):
+           cf, g, zt, x, send, recv, ab, ro, at, lh, lt, us, tau, w, ev, ob, o32, ssem, rsem, offs, offr, osem):
     gx, gy = lax.axis_index("gx"), lax.axis_index("gy")
     me = gx * 16 + gy
     comm = "comm" in parts
@@ -73,49 +72,73 @@
     ev[pl.ds(0, 64), :] = jnp.concatenate([re, im], axis=1).astype(BF16)
     ev[pl.ds(64, 64), :] = jnp.concatenate([-im, re], axis=1).astype(BF16)
 
+    none = jnp.zeros((8, 128), F32)
+    top = jnp.concatenate([nodes_ref[...], none], axis=1)
+    bottom = jnp.concatenate([none, nodes_ref[...]], axis=1)
+    us[...] = jnp.zeros((8, 128, 256), BF16)
+    for p in range(8):
+        us[p, pl.ds(16 * p, 16), :] = jnp.concatenate([top, bottom], axis=0).astype(BF16)
+
     for m in range(64):
         ab[m] = off_ref[0, :, pl.ds(m * 128, 128)].astype(F32)
-    for k in range(2):
-        rows = ab[:, k, :]
-        at[k] = jnp.concatenate([rows, rows], axis=0).T
-        at[2 + k, pl.ds(0, 64)] = rows
-
     lane = lax.broadcasted_iota(jnp.int32, (16, 128), 1)
     low = lane < 64
-    ui = nodes_ref[0:1, :]
-    uj = nodes_ref[1:2, :]
-    quarter = jnp.where(low, 0.0, -0.25).astype(F32)
-
-    def column(ref, k, row, j):
-        return jnp.broadcast_to(pltpu.roll(ref[k, pl.ds(row, 16), :], (128 - j) & 127, 1)[:, 0:1], (16, 128))
-
-    def many_phases(total, place, offset_of, first, count):
-        @pl.loop(0, total, step=TILES)
+    signed = jnp.where(low, 0.25, -0.25).astype(F32)
+    wide = lax.broadcasted_iota(jnp.int32, (64, 128), 1) < 64
+
+    def make_tau(oa, ob_):
+        for k in range(3):
+            lh[pl.ds(2 * k, 64, stride=8), :] = oa
+            lh[pl.ds(2 * k + 1, 64, stride=8), :] = ob_
+        for k in range(6, 8):
+            lh[pl.ds(k, 64, stride=8), :] = jnp.zeros((64, 128), F32)
+        for n in range(4):
+            lt[pl.ds(n * 128, 128), :] = lh[pl.ds(n * 128, 128), :].T.astype(BF16)
+
+        @pl.loop(0, 8, step=2)
+        def _(p):
+            for e in range(2):
+                r = jnp.dot(lt[...], us[p + e], preferred_element_type=F32)
+                for n in range(4):
+                    row = pl.multiple_of((n * 16 + 2 * (p + e)) * 128, 128)
+                    tau[pl.ds(row, 128), :] = r[n * 128:n * 128 + 128, 0:128]
+                    tau[pl.ds(row + 128, 128), :] = r[n * 128:n * 128 + 128, 128:256]
+
+    def start(t, first):
+        c1 = cosine_turns(t)
+        s1 = cosine_turns(t + signed)
+        twice = 2.0 * c1
+        if first == 1:
+            return (c1, s1), (1.0, 0.0), twice
+        c2, s2 = twice * c1 - 1.0, twice * s1
+        if first == 8:
+            k2 = 2.0 * c2
+            c4, s4 = k2 * c2 - 1.0, k2 * s2
+            k4 = 2.0 * c4
+            c8, s8 = k4 * c4 - 1.0, k4 * s4
+            return (c8, s8), (c8 * c1 + s8 * s1, s8 * c1 - c8 * s1), twice
+        c3, s3 = twice * c2 - c1, twice * s2 - s1
+        k3 = 2.0 * c3
+        c6, s6 = k3 * c3 - 1.0, k3 * s3
+        c7, s7 = c6 * c1 - s6 * s1, s6 * c1 + c6 * s1
+        k7 = 2.0 * c7
+        c14, s14 = k7 * c7 - 1.0, k7 * s7
+        return (c14, s14), (c14 * c1 + s14 * s1, s14 * c1 - c14 * s1), twice
+
+    def phase_tiles(i, slot, first, count, j, tiles):
+        state = [start(tau[pl.ds((j + n) * 64 + i * 16, 16), :], first) for n in range(tiles)]
+        for l in range(count):
+            for n in range(tiles):
+                now, before, twice = state[n]
+                zt[slot, l, j + n, :, pl.ds(0, 128)] = now[0].astype(BF16)
+                zt[slot, l, j + n, :, pl.ds(128, 128)] = now[1].astype(BF16)
+                if l + 1 < count:
+                    state[n] = ((twice * now[0] - before[0], twice * now[1] - before[1]), now, twice)
+
+    def many_phases(i, slot, first, count):
+        @pl.loop(0, 128, step=TILES)
         def _(j):
-            spots = [place(j + u) for u in range(TILES)]
-            state = []
-            for u in range(TILES):
-                a, b = offset_of(j + u)
-                tau = a * ui + b * uj
-                if first == 1:
-                    now = cosine_turns(tau + quarter)
-                    twice = 2.0 * jnp.where(low, now, pltpu.roll(now, 64, 1))
-                    before = jnp.where(low, 1.0, 0.0).astype(F32)
-                else:
-                    twice = 2.0 * cosine_turns(tau)
-                    now = cosine_turns(tau * float(first) + quarter)
-                    before = cosine_turns(tau * float(first - 1) + quarter)
-                state.append((now, before, twice))
-            for l in range(count):
-                for u in range(TILES):
-                    now, before, twice = state[u]
-                    i, q = spots[u]
-                    zb = now.astype(BF16)
-                    rb = swap(zb)
-                    zt[i, l, q, :, pl.ds(0, 128)] = jnp.where(low, zb, rb)
-                    zt[i, l, q, :, pl.ds(128, 128)] = jnp.where(low, -rb, zb)
-                    if l + 1 < count:
-                        state[u] = (twice * now - before, now, twice)
+            phase_tiles(i, slot, first, count, j, TILES)
 
     def turned(tile, i, l, q):
         return tile * zt[i, l, q, :, pl.ds(0, 128)] + swap(tile) * zt[i, l, q, :, pl.ds(128, 128)]
@@ -140,22 +163,28 @@
     def save_x(q, v):
         x[q] = v.astype(BF16)
 
+    pair = []
+    for k in range(2):
+        rows = ab[:, k, :]
+        at[...] = jnp.concatenate([rows, rows], axis=0).T
+        pair.append(jnp.where(wide, at[pl.ds(0, 64, stride=2), :], at[pl.ds(1, 64, stride=2), :]))
+    make_tau(*pair)
+
     @pl.loop(0, 8)
     def _(j):
         cf[pl.ds(j * 1024, 1024), :] = ch_ref[0, pl.ds(j * 1024, 1024), :].astype(F32)
 
     @pl.loop(0, 4)
     def _(i):
-        @pl.loop(0, 128)
-        def _(q):
+        @pl.loop(0, 128, step=TILES)
+        def _(j):
+            if "z1" in parts:
+                phase_tiles(i, i, 1, 7, j, TILES)
             if "gather" in parts:
-                base = i * 2048 + q
-                for s in range(16):
-                    slot = slot_ref[0, base + s * 128]
-                    g[i, q, pl.ds(s, 1), :] = cf[pl.ds(slot, 1), :]
-
-        if "z1" in parts:
-            many_phases(128, lambda j: (i, j), lambda j: (column(at, 2, i * 16, j), column(at, 3, i * 16, j)), 1, 7)
+                for n in range(TILES):
+                    for r in range(16):
+                        slot = slot_ref[0, (i * 16 + r) * 128 + j + n]
+                        g[i, j + n, pl.ds(r, 1), :] = cf[pl.ds(slot, 1), :]
 
     if "p1" in parts:
         @pl.loop(0, 4)
@@ -167,7 +196,7 @@
                 else:
                     def save(q, v):
                         c, t, hi = (q >> 4) & 3, q & 15, q >> 6
-                        cf[pl.ds(((c * 64 + 16 * i) * 2 + hi) * 16 + t, 16, stride=32), :] = v
+                        cf[pl.ds((c * 64 + 16 * i) * 33 + hi * 16 + t, 16, stride=33), :] = v
                 level(i, l, l, load, save)
 
     if comm:
@@ -180,14 +209,15 @@
                                          recv_sem=offr.at[0], device_id=(dst >> 4, dst & 15), device_id_type=MESH).start()
         pltpu.make_async_copy(ab.at[me >> 1], ro.at[me], offr.at[0]).start()
 
+    make_tau(ab[:, 0, :], ab[:, 1, :])
+
     @pl.loop(0, 4)
     def _(c):
         if "z2" in parts:
-            many_phases(128, lambda j: (0, j), lambda j: (
-                column(at, 0, (j & 1) * 64 + c * 16, j >> 1), column(at, 1, (j & 1) * 64 + c * 16, j >> 1)), 8, 6)
+            many_phases(c, 0, 8, 6)
         if "p2" in parts:
             for l in range(6):
-                load = load_x if l > 0 else (lambda q: cf[pl.ds((c * 128 + q) * 16, 16), :].astype(BF16))
+                load = load_x if l > 0 else (lambda q: cf[pl.ds((c * 64 + (q >> 1)) * 33 + (q & 1) * 16, 16), :].astype(BF16))
                 if l < 5:
                     save = save_x
                 else:
@@ -204,15 +234,19 @@
 
     if comm:
         pltpu.make_async_copy(ro, ro, offr.at[0]).wait()
+    odd = jnp.full((64, 128), me & 1, jnp.int32) == 1
+    pair = []
     for k in range(2):
-        at[k] = ro[:, k, :].T
-    half = (me & 1) * 64
+        first, second = ro[pl.ds(0, 64, stride=2), k, :], ro[pl.ds(1, 64, stride=2), k, :]
+        even_half = jnp.where(wide, first, pltpu.roll(second, 64, 1))
+        odd_half = jnp.where(wide, pltpu.roll(first, 64, 1), second)
+        pair.append(jnp.where(odd, odd_half, even_half))
+    make_tau(*pair)
 
     if "z3" in parts:
         @pl.loop(0, 4)
         def _(c):
-            row = pl.multiple_of(half + c * 16, 16)
-            many_phases(128, lambda j: (c, j), lambda j: (column(at, 0, row, j), column(at, 1, row, j)), 14, 8)
+            many_phases(c, c, 14, 8)
 
     @pl.loop(0, 4)
     def _(c):
@@ -225,9 +259,9 @@
                 rows = jnp.concatenate([turned(x[q], c, 7, q) for q in range(blk * 32, blk * 32 + 32)], axis=0)
                 v = jnp.dot(rows, ev[...], preferred_element_type=F32)
                 for j in range(32):
-                    o32[pl.ds(blk * 32 + j, 16, stride=128), :] = v[16 * j:16 * j + 16]
+                    o32[pl.ds(blk * 32 + j, 16, stride=129), :] = v[16 * j:16 * j + 16]
             for t in range(16):
-                ob[c, t] = o32[pl.ds(t * 128, 128), :].astype(BF16)
+                ob[c, t] = o32[pl.ds(t * 129, 128), :].astype(BF16)
         pltpu.make_async_copy(ob.at[c], out_ref.at[pl.ds(c * 16, 16)], osem.at[c]).start()
 
     for c in range(4):
@@ -243,10 +277,14 @@
     u = np.cos(math.pi * (2.0 * np.arange(side) + 1.0) / (2.0 * side))
     row = np.repeat(u, side)
     col = np.tile(u, side)
-    table = np.zeros((8, 128))
-    table[0] = np.concatenate([row, row]) / TURN
-    table[1] = np.concatenate([col, col]) / TURN
-    return table.astype(np.float32)
+    table = np.zeros((8, 128), np.float32)
+    left = [np.concatenate([row, row]) / TURN, np.concatenate([col, col]) / TURN]
+    for k in range(3):
+        for n in range(2):
+            part = left[n].astype(np.float32).astype(jnp.bfloat16).astype(np.float64)
+            table[2 * k + n] = part
+            left[n] = left[n] - part
+    return table
 
 
 def body(charges, leaf_slot, node_offset, lagrange, evaluate, parts=PARTS):
@@ -259,7 +297,7 @@
         in_specs=[vm, pl.BlockSpec(memory_space=pltpu.SMEM), vm, vm, vm, vm],
         out_specs=pl.BlockSpec(memory_space=pl.ANY),
         scratch_shapes=[
-            pltpu.VMEM((8192, 128), F32),
+            pltpu.VMEM((256 * 33, 128), F32),
             pltpu.VMEM((4, 128, 16, 128), F32),
             pltpu.VMEM((4, 8, 128, 16, 256), BF16),
             pltpu.VMEM((128, 16, 128), BF16),
@@ -267,11 +305,15 @@
             pltpu.VMEM((4, 128, 16, 128), BF16),
             pltpu.VMEM((64, 2, 128), F32),
             pltpu.VMEM((128, 2, 128), F32),
-            pltpu.VMEM((4, 128, 128), F32),
+            pltpu.VMEM((128, 128), F32),
+            pltpu.VMEM((512, 128), F32),
+            pltpu.VMEM((512, 128), BF16),
+            pltpu.VMEM((8, 128, 256), BF16),
+            pltpu.VMEM((8192, 128), F32),
             pltpu.VMEM((256, 256), BF16),
             pltpu.VMEM((128, 128), BF16),
             pltpu.VMEM((4, 16, 128, 128), BF16),
-            pltpu.VMEM((2048, 128), F32),
+            pltpu.VMEM((16 * 129, 128), F32),
             pltpu.SemaphoreType.DMA((4,)), pltpu.SemaphoreType.DMA((4,)),
             pltpu.SemaphoreType.DMA((1,)), pltpu.SemaphoreType.DMA((1,)), pltpu.SemaphoreType.DMA((4,)),
         ],

time: 131 us -> 88.6 us (0.68)
  Pallas kernels: 128 us -> 85.3 us
    pallas_call x1, Pallas kernels: 128 us -> 85.3 us  [body(): pl.pallas_call(functools.partial(kernel, parts), out_shape=jax.ShapeDtype...]
where the time goes in v2:
time: 88.6 us; the launch traced here: 88.5 us
  Pallas kernels  85.3 us (96%)
  local copies, waits for them, and re-layouts  3.16 us (4%)
    pallas_call x1, Pallas kernels, body(): pl.pallas_call(functools.partial(kernel, parts), out_shape=jax.ShapeDtype...  85.3 us
    unnamed x1, local copies, waits for them, and re-layouts  3.16 us

profile of v2, /device:TPU:1, one launch (start us, length us, event | category | flops | bytes accessed | tf_op | source)
XLA Modules:
  0.0 88.5 jit_solution(7527302457023964634)
XLA Ops:
  0.0 85.3 %shard_map.64 = bf16[64,128,128]{2,1,0:T(8,128)(2,1)} custom-call(bf16[1,8192,128]{2,1,0:T(8,128)(2,1)} %ch_ref.1, s32[1,8192]{1,0:T(1,128)} %slot_ref.1, bf16[1,2,8192]{2,1,0:T(2,128)(2,1)} %off_ref.1, bf16[2,2,2,64,64]{4,3,2,1,0:T(8,128)(2,1)} %lag_ref.1, bf16[2,64,64]{2,1,0:T(8,128)(2,1)} %ev_ref.1, f32[8,128]{1,0:T(8,128)} %constant.2.clone.nodes_ref), custom_call_target="tpu_custom_call" | custom-call | tf_op jit(solution)/shard_map/pallas_call | solution.py:294
  85.3 3.2 %copy.8 = bf16[64,128,128]{2,1,0:T(8,128)(2,1)} copy(bf16[64,128,128]{2,1,0:T(8,128)(2,1)} %shard_map.64) | data formatting | bytes 4194304

commit v3 on v2

--- a/solution.py
+++ b/solution.py
@@ -56,10 +56,13 @@
     if comm:
         bar = pltpu.get_barrier_semaphore()
 
-        @pl.loop(1, 128)
-        def _(k):
+        def greet(k):
             dst = (me + k) & 127
             pl.semaphore_signal(bar, inc=1, device_id=(dst >> 4, dst & 15), device_id_type=MESH)
+
+        @pl.loop(1, 16)
+        def _(k):
+            greet(k)
 
     for e in range(2):
         for c in range(2):
@@ -178,6 +181,8 @@
     def _(i):
         @pl.loop(0, 128, step=TILES)
         def _(j):
+            if comm:
+                greet(16 + i * 16 + j // 8)
             if "z1" in parts:
                 phase_tiles(i, i, 1, 7, j, TILES)
             if "gather" in parts:
@@ -189,6 +194,8 @@
     if "p1" in parts:
         @pl.loop(0, 4)
         def _(i):
+            for n in range(12 if comm else 0):
+                greet(80 + i * 12 + n)
             for l in range(7):
                 load = load_x if l > 0 else (lambda q: g[i, q].astype(BF16))
                 if l < 6:

time: 88.6 us -> 92.9 us (1.049)
  Pallas kernels: 85.3 us -> 89.6 us
    pallas_call x1, Pallas kernels: 85.3 us -> 89.6 us  [body(): pl.pallas_call(functools.partial(kernel, parts), out_shape=jax.ShapeDtype...]
where the time goes in v3:
time: 92.9 us; the launch traced here: 92.8 us
  Pallas kernels  89.6 us (96%)
  local copies, waits for them, and re-layouts  3.16 us (3%)
    pallas_call x1, Pallas kernels, body(): pl.pallas_call(functools.partial(kernel, parts), out_shape=jax.ShapeDtype...  89.6 us
    unnamed x1, local copies, waits for them, and re-layouts  3.16 us

profile of v3, /device:TPU:1, one launch (start us, length us, event | category | flops | bytes accessed | tf_op | source)
XLA Modules:
  0.0 92.8 jit_solution(15051154506604038216)
XLA Ops:
  0.0 89.6 %shard_map.64 = bf16[64,128,128]{2,1,0:T(8,128)(2,1)} custom-call(bf16[1,8192,128]{2,1,0:T(8,128)(2,1)} %ch_ref.1, s32[1,8192]{1,0:T(1,128)} %slot_ref.1, bf16[1,2,8192]{2,1,0:T(2,128)(2,1)} %off_ref.1, bf16[2,2,2,64,64]{4,3,2,1,0:T(8,128)(2,1)} %lag_ref.1, bf16[2,64,64]{2,1,0:T(8,128)(2,1)} %ev_ref.1, f32[8,128]{1,0:T(8,128)} %constant.2.clone.nodes_ref), custom_call_target="tpu_custom_call" | custom-call | tf_op jit(solution)/shard_map/pallas_call | solution.py:301
  89.6 3.2 %copy.8 = bf16[64,128,128]{2,1,0:T(8,128)(2,1)} copy(bf16[64,128,128]{2,1,0:T(8,128)(2,1)} %shard_map.64) | data formatting | bytes 4194304
